TPU v7x, 512 devices: a whole 4x8x8 slice. The times are simulated.
512 devices in a mesh: row: 64 (over z, y), col: 2 (over core), rhs: 4 (over x).
Axes of the slice: x: 4, y: 8, z: 8, core: 2. Of those that a mesh axis runs over, the one named last changes fastest.
Arguments:
- factor: float32 [2, 131072, 2048], P(None, 'row', 'col'), may hold values from -0.125 to 0.125
- inverses: float32 [2, 2048, 2048], P(None, 'col'), may hold values from -0.125 to 0.125
- rhs: float32 [131072, 512], P('row', 'rhs'), may hold values from -6 to 6
Outputs:
- solution: float32 [2, 2048, 512], P(None, 'col', 'rhs')
- updated: float32 [131072, 512], P(('row', 'col'), 'rhs')
All inputs are finite; a program needn't handle non-finite values.
Results may differ from a plain program's by a relative error of at most 0.000084.
Values sent between devices are 32-bit elements; how exact they have to be, the bound alone decides.
A program may use at most 128 MiB of HBM per device.

v0:
```python
import jax
import jax.numpy as jnp
from jax import lax
from jax.sharding import PartitionSpec as P


def broadcast(block, axis, owner):
    block = jnp.where(lax.axis_index(axis) == owner, block, jnp.zeros_like(block))
    return lax.psum(block, axis)


def body(factor, inverses, rhs):
    precise = lax.Precision.HIGHEST
    n_rows = lax.axis_size("row")
    row_pos = lax.axis_index("row")
    col_pos = lax.axis_index("col")
    block_size = inverses.shape[2]
    local_rows = rhs.shape[0]
    per_dev = local_rows // block_size
    block_ids = jnp.repeat(jnp.arange(per_dev, dtype=jnp.int32) * n_rows + row_pos, block_size)

    def share_solved(step_index, local_piece):
        return broadcast(local_piece, "row", step_index % n_rows)

    first_solution = share_solved(
        0, jnp.dot(inverses[0], rhs, precision=precise, preferred_element_type=jnp.float32)
    )
    head_mask = (block_ids > 0)[:, None]
    head_term = jnp.where(
        head_mask,
        jnp.dot(factor[0], first_solution, precision=precise, preferred_element_type=jnp.float32),
        0.0,
    )
    summed = lax.psum(head_term, "col")
    local_second = jnp.dot(
        inverses[1], rhs - summed, precision=precise, preferred_element_type=jnp.float32
    )
    second_solution = share_solved(1, local_second)
    tail_term = jnp.where(
        (block_ids[block_size:] > 0)[:, None],
        jnp.dot(
            factor[0][block_size:],
            first_solution,
            precision=precise,
            preferred_element_type=jnp.float32,
        ),
        0.0,
    )
    first_full = jnp.concatenate([head_term, tail_term], axis=0)
    combined = first_full + jnp.where(
        (block_ids > 1)[:, None],
        jnp.dot(factor[1], second_solution, precision=precise, preferred_element_type=jnp.float32),
        0.0,
    )
    share_rows = local_rows // lax.axis_size("col")
    reduced = lax.psum_scatter(combined, "col", scatter_dimension=0, tiled=True)
    own_rows = lax.dynamic_slice_in_dim(rhs, col_pos * share_rows, share_rows, 0)
    return (jnp.stack([first_solution, second_solution]), own_rows - reduced)


def solution(mesh):
    in_specs = (P(None, "row", "col"), P(None, "col", None), P("row", "rhs"))
    out_specs = (P(None, "col", "rhs"), P(("row", "col"), "rhs"))
    return jax.shard_map(body, mesh=mesh, in_specs=in_specs, out_specs=out_specs, check_vma=False)
```

profile of v0, /device:TPU:57, one launch (start us, length us, event | category | flops | bytes accessed | tf_op | source)
XLA Modules:
  0.0 427.8 jit_solution(11225290273483708096)
XLA Ops:
  7.2 0.0 copy-start
  7.2 0.0 all-reduce.4.cloned.1.call-start
  7.2 11.0 %fusion.27 = f32[1024,128]{1,0:T(8,128)} fusion(f32[2048,128]{1,0:T(8,128)} %param.5, f32[2,1024,2048]{2,1,0:T(8,128)} %param.4, pred[]{:T(512)S(6)} %eq.6), kind=kOutput, calls=%fused_computation.17 | convolution fusion | flops 3221356544 | bytes 9961473 | tf_op jit(solution)/shard_map/dot_general | solution.py:26
  18.3 0.0 all-reduce.4.cloned.1.call-update
  18.3 0.0 all-reduce.6.cloned.1.call-start
  18.3 155.0 %all-reduce.4.cloned.1.call-done = f32[1024,128]{1,0:T(8,128)} async-done(((f32[1024,128]{1,0:T(8,128)}), f32[1024,128]{1,0:T(8,128)}) %all-reduce.4.cloned.1.call-update) | async-done | bytes 524304 | tf_op jit(solution)/shard_map/psum | solution.py:9
  173.3 0.0 copy-start.1
  173.3 13.4 %fusion.15 = f32[2048,128]{0,1:T(8,128)} fusion(f32[1024,128]{1,0:T(8,128)} %all-reduce.4.cloned.1.call-done, f32[2,2048,1024]{2,1,0:T(8,128)} %param.3, pred[]{:T(512)S(6)} %gt.10), kind=kOutput, calls=%fused_computation.13 | convolution fusion | flops 3221487616 | bytes 9961473 | tf_op jit(solution)/shard_map/dot_general | solution.py:31
  186.7 0.0 all-reduce.6.cloned.1.call-update
  186.7 0.2 all-reduce.8.cloned.1.call-start
  186.9 0.0 copy-done
  186.9 0.3 copy.5
  187.3 37.6 %all-reduce.6.cloned.1.call-done = f32[2048,128]{0,1:T(8,128)} async-done(((f32[2048,128]{0,1:T(8,128)}), f32[2048,128]{0,1:T(8,128)}) %all-reduce.6.cloned.1.call-update) | async-done | bytes 1048592 | tf_op jit(solution)/shard_map/psum | solution.py:34
  224.8 10.0 %fusion.33 = f32[1024,128]{1,0:T(8,128)} fusion(f32[2,1024,2048]{2,1,0:T(8,128)} %param.4, f32[2048,128]{0,1:T(8,128)S(1)} %copy.5, f32[2048,128]{0,1:T(8,128)} %all-reduce.6.cloned.1.call-done, pred[]{:T(512)S(6)} %eq.7), kind=kOutput, calls=%fused_computation.19 | convolution fusion | flops 3221618688 | bytes 11010049 | tf_op jit(solution)/shard_map/dot_general | solution.py:35
  234.9 0.0 all-reduce.8.cloned.1.call-update
  234.9 0.0 reduce-scatter.2.cloned.1.call-start
  235.0 151.9 %all-reduce.8.cloned.1.call-done = f32[1024,128]{1,0:T(8,128)} async-done(((f32[1024,128]{1,0:T(8,128)}), f32[1024,128]{1,0:T(8,128)}) %all-reduce.8.cloned.1.call-update) | async-done | bytes 524304 | tf_op jit(solution)/shard_map/psum | solution.py:9
  386.8 13.5 %fusion.24 = f32[2048,128]{0,1:T(8,128)} fusion(f32[2048,128]{0,1:T(8,128)} %fusion.15, f32[1024,128]{1,0:T(8,128)} %all-reduce.8.cloned.1.call-done, f32[2,2048,1024]{2,1,0:T(8,128)} %param.3, pred[]{:T(512)S(6)} %gt.11), kind=kOutput, calls=%fused_computation.16 | convolution fusion | flops 3221749760 | bytes 11010049 | tf_op jit(solution)/shard_map/dot_general | solution.py:52
  400.4 0.0 reduce-scatter.2.cloned.1.call-update
  400.4 0.0 copy-done.1
  400.4 2.1 pad_maximum_fusion
  402.5 16.7 %reduce-scatter.2.cloned.1.call-done = f32[1024,128]{0,1:T(8,128)} async-done(((f32[2048,128]{0,1:T(8,128)}), f32[1024,128]{0,1:T(8,128)}) %reduce-scatter.2.cloned.1.call-update) | async-done | bytes 524304 | tf_op jit(solution)/shard_map/reduce_scatter | solution.py:56
  419.2 1.1 dynamic-slice_subtract_fusion
  420.3 1.0 copy.8
Async XLA Ops:
  7.2 179.8 %copy-start = (f32[2048,128]{1,0:T(8,128)S(1)}, f32[2048,128]{1,0:T(8,128)}, u32[]{:S(2)}) copy-start(f32[2048,128]{1,0:T(8,128)} %param.5) | copy-start | bytes 3145732
  7.2 166.1 %all-reduce.4.cloned.1.call-start = ((), (), s32[]{:S(2)}) async-start(), calls=%async_computation.1 | async-start | bytes 1048576 | tf_op jit(solution)/shard_map/psum | solution.py:9
  18.3 206.6 %all-reduce.6.cloned.1.call-start = ((), (), s32[]{:S(2)}) async-start(), calls=%async_computation.2 | async-start | bytes 2097152 | tf_op jit(solution)/shard_map/psum | solution.py:34
  173.3 227.1 %copy-start.1 = (f32[1024,128]{1,0:T(8,128)S(1)}, f32[1024,128]{1,0:T(8,128)}, u32[]{:S(2)}) copy-start(f32[1024,128]{1,0:T(8,128)} %all-reduce.4.cloned.1.call-done) | copy-start | bytes 1572868
  186.7 200.1 %all-reduce.8.cloned.1.call-start = ((), (), s32[]{:S(2)}) async-start(), calls=%async_computation.3 | async-start | bytes 1048576 | tf_op jit(solution)/shard_map/psum | solution.py:9
  234.9 184.3 %reduce-scatter.2.cloned.1.call-start = ((), (), s32[]{:S(2)}) async-start(), calls=%async_computation.4 | async-start | bytes 1572864 | tf_op jit(solution)/shard_map/reduce_scatter | solution.py:56
Sparse Core Ops, SparseCore 0:
  18.4 154.8 all-reduce.3
  186.8 37.9 all-reduce.5
  235.0 151.7 all-reduce.7
  400.5 18.6 reduce-scatter.1
where the time goes:
time: 430 us; the launch traced here: 428 us
  waiting for transfers between devices  361 us (84%)
  matrix products  48 us (11%)
  between operations  13.8 us (3%)
    psum x2, waiting for transfers between devices, broadcast(): return lax.psum(block, axis)  307 us
    psum x1, waiting for transfers between devices, body(): summed = lax.psum(head_term, 'col')  37.6 us
    reduce_scatter x1, waiting for transfers between devices, body(): reduced = lax.psum_scatter(combined, 'col', scatter_dimension=0, tiled=True)  16.7 us
    dot_general x1, matrix products, body(): jnp.dot(factor[1], second_solution, precision=precise, preferred_element_...  13.5 us
    dot_general x1, matrix products, body(): jnp.dot(factor[0], first_solution, precision=precise, preferred_element_t...  13.4 us
    dot_general x1, matrix products, body(): jnp.dot(inverses[0], rhs, precision=precise, preferred_element_type=jnp.f...  11 us
    dot_general x1, matrix products, body(): jnp.dot(inverses[1], rhs - summed, precision=precise, preferred_element_t...  10 us
  transfers between devices with their start and end apart: 4, of which 4 were waited for; matrix products, arithmetic and copies ran while one was open for 1% of the time, Pallas kernels for 0%

commit v1 on v0

v1 whole, which is shorter than its diff:
```python
import functools

import jax
import jax.numpy as jnp
from jax import lax
from jax.experimental import pallas as pl
from jax.experimental.pallas import tpu as pltpu
from jax.sharding import PartitionSpec as P

MESH = pl.DeviceIdType.MESH
F32 = jnp.float32
BF16 = jnp.bfloat16
SIDE = 8
FAR_FIRST = (4, 3, 5, 2, 6, 1, 7)
HALF = 512
PIECE = 64
LANES = 128
MIB = 1 << 20


def split(value):
    high = value.astype(BF16)
    return high, (value - high.astype(F32)).astype(BF16)


def kernel(
    factor, inverses, rhs, solved_out, updated_out,
    first_low, second_low, inverse_low, stage, stage_wide, b, x0, x1, w0, w1, wide, acc, other, detour,
    stage_sem, b_sem, piece_sem, scatter_sem, along_sem, across_sem, direct_sem, direct_send,
    detour_sem, detour_send, forward_send, swap_sem, swap_send, out_sem,
):
    row = lax.axis_index("row")
    col = lax.axis_index("col")
    y = lax.rem(row, SIDE)
    z = lax.div(row, SIDE)
    sibling = {"col": 1 - col}
    is_first = row == 0
    is_second = row == 1
    is_detour = (row == SIDE) | (row == 7 * SIDE)
    pending = []

    def load(matrix, index, block, rows, buffer, slot):
        return pltpu.make_async_copy(
            matrix.at[index, pl.ds(pl.multiple_of(block * rows, rows), rows)], buffer.at[slot], stage_sem.at[slot]
        )

    def prime(matrix, index, rows, buffer):
        for slot in range(4):
            load(matrix, index, slot, rows, buffer, slot).start()

    def split_block(matrix, index, rows, buffer, target, width, block, blocks):
        slot = lax.rem(block, 4)
        load(matrix, index, block, rows, buffer, slot).wait()

        def part(k, _):
            at = pl.multiple_of(k * 16, 16)
            high, low = split(buffer[slot, pl.ds(at, 16), :])
            to = pl.ds(pl.multiple_of(block * rows + at, 16), 16)
            target[to, :width] = high
            target[to, width:] = low
            return 0

        lax.fori_loop(0, rows // 16, part, 0)

        @pl.when(block + 4 < blocks)
        def _():
            load(matrix, index, block + 4, rows, buffer, slot).start()

    def split_factor(index, target):
        def step(block, _):
            split_block(factor, index, 256, stage, target, 1024, block, 8)
            return 0
        lax.fori_loop(0, 8, step, 0)

    def split_inverse(index, begin, count):
        def step(block, _):
            split_block(inverses, index, 128, stage_wide, inverse_low, 2048, block, 8)
            return 0
        lax.fori_loop(begin, begin + count, step, 0)

    def spread(value, target, at, rows, depth):
        high, low = split(value)
        for base in (0, depth):
            target[pl.ds(pl.multiple_of(base + at, 16), rows), :LANES] = high
            target[pl.ds(pl.multiple_of(base + at, 16), rows), LANES:] = low

    def spread_all(source, target, depth):
        def step(k, _):
            at = pl.multiple_of(k * 64, 64)
            spread(source[pl.ds(at, 64), :], target, at, 64, depth)
            return 0
        lax.fori_loop(0, depth // 64, step, 0)

    def product(matrix, at, rows, weights):
        both = jnp.dot(matrix[pl.ds(pl.multiple_of(at, rows), rows), :], weights[...], preferred_element_type=F32)
        return both[:, :LANES] + both[:, LANES:]

    b_copy = pltpu.make_async_copy(rhs, b, b_sem)
    b_copy.start()

    @pl.when(is_first)
    def _():
        prime(inverses, 0, 128, stage_wide)

    @pl.when(jnp.logical_not(is_first))
    def _():
        prime(factor, 0, 256, stage)

    def at(yy, zz):
        return {"row": zz * SIDE + yy}

    barrier = pltpu.get_barrier_semaphore()
    for k in range(1, SIDE):
        pl.semaphore_signal(barrier, inc=1, device_id=at(lax.rem(y + k, SIDE), z), device_id_type=MESH)
        pl.semaphore_signal(barrier, inc=1, device_id=at(y, lax.rem(z + k, SIDE)), device_id_type=MESH)
    pl.semaphore_signal(barrier, inc=1, device_id=sibling, device_id_type=MESH)

    @pl.when(is_second)
    def _():
        for k in (1, 7):
            pl.semaphore_signal(barrier, inc=1, device_id={"row": k * SIDE}, device_id_type=MESH)

    def pass_barrier():
        @pl.when(is_detour)
        def _():
            pl.semaphore_wait(barrier, 16)

        @pl.when(jnp.logical_not(is_detour))
        def _():
            pl.semaphore_wait(barrier, 15)

    def rows_of(half, index):
        return pl.ds(pl.multiple_of(half * HALF + index * PIECE, PIECE), PIECE)

    def send(condition, buffer, rows, target, send_sem, recv_sem):
        copy = pltpu.make_async_remote_copy(
            src_ref=buffer.at[rows], dst_ref=buffer.at[rows], send_sem=send_sem, recv_sem=recv_sem,
            device_id=target, device_id_type=MESH,
        )

        @pl.when(condition)
        def _():
            copy.start()

        pending.append((condition, copy))

    def scatter(which, buffer, half, index, holds):
        owner = which
        place = index if half == 0 else index * SIDE + owner
        if place == owner or place in holds:
            return
        send(row == owner, buffer, rows_of(half, index), {"row": place},
             scatter_sem.at[which, half, index], piece_sem.at[which, half, index])

    def has_all(holds):
        return functools.reduce(jnp.logical_or, [row == q for q in holds])

    def arrive(which, buffer, half, index, holds):
        @pl.when(jnp.logical_not(has_all(holds)))
        def _():
            part = buffer.at[rows_of(half, index)]
            pltpu.make_async_copy(part, part, piece_sem.at[which, half, index]).wait()

    def relay(which, buffer, holds, wait):
        owner_y = which
        for half in range(2):
            mine, cross, cross_owner = (y, z, 0) if half == 0 else (z, y, owner_y)
            if wait:
                arrive(which, buffer, half, mine, holds)
            for k in FAR_FIRST:
                there = lax.rem(cross + k, SIDE)
                target = y + there * SIDE if half == 0 else z * SIDE + there
                skip = functools.reduce(jnp.logical_or, [target == q for q in holds])
                send((cross == cross_owner) & jnp.logical_not(skip), buffer, rows_of(half, mine), {"row": target},
                     along_sem.at[which, half, k], piece_sem.at[which, half, mine])
            for k in FAR_FIRST:
                there = lax.rem(mine + k, SIDE)
                target = z * SIDE + there if half == 0 else y + there * SIDE
                skip = functools.reduce(jnp.logical_or, [target == q for q in holds])
                send(jnp.logical_not(skip), buffer, rows_of(half, mine), {"row": target},
                     across_sem.at[which, half, k], piece_sem.at[which, half, mine])

    def collect(which, buffer, holds):
        for k in (1, 7, 2, 6, 3, 5, 4):
            arrive(which, buffer, 0, lax.rem(y + k, SIDE), holds)
            arrive(which, buffer, 1, lax.rem(z + k, SIDE), holds)

    holds0, holds1 = (0, 1), (1,)

    def direct(block):
        return pltpu.make_async_remote_copy(
            src_ref=x0.at[pl.ds(block * 256, 128)], dst_ref=x0.at[pl.ds(block * 256, 128)],
            send_sem=direct_send.at[block], recv_sem=direct_sem.at[block], device_id={"row": 1}, device_id_type=MESH)

    def aside(block, way):
        return pltpu.make_async_remote_copy(
            src_ref=x0.at[pl.ds(block * 256 + 128 + way * 64, 64)], dst_ref=detour.at[pl.ds(block * 64, 64)],
            send_sem=detour_send.at[block, way], recv_sem=detour_sem.at[block],
            device_id={"row": (SIDE, 7 * SIDE)[way]}, device_id_type=MESH)

    def forward(block, way):
        return pltpu.make_async_remote_copy(
            src_ref=detour.at[pl.ds(block * 64, 64)], dst_ref=x0.at[pl.ds(block * 256 + 128 + way * 64, 64)],
            send_sem=forward_send.at[block], recv_sem=direct_sem.at[4 + block * 2 + way],
            device_id={"row": 1}, device_id_type=MESH)

    @pl.when(is_first)
    def _():
        b_copy.wait()
        spread_all(b, wide, 2048)
        for block in range(4):
            split_inverse(0, 2 * block, 2)
            x0[pl.ds(block * 256, 256), :] = product(inverse_low, block * 256, 256, wide)
            if block == 0:
                pass_barrier()
            direct(block).start()
            for way in range(2):
                aside(block, way).start()

    @pl.when(jnp.logical_not(is_first))
    def _():
        b_copy.wait()
        split_factor(0, first_low)
        pass_barrier()

    for half in range(2):
        for index in range(SIDE):
            scatter(0, x0, half, index, holds0)

    for way in range(2):
        @pl.when(row == (SIDE, 7 * SIDE)[way])
        def _():
            for block in range(4):
                part = detour.at[pl.ds(block * 64, 64)]
                pltpu.make_async_copy(part, part, detour_sem.at[block]).wait()
                forward(block, way).start()

    def swap(block):
        rows = pl.ds(pl.multiple_of(block * 512, 512), 512)
        return rows, pltpu.make_async_remote_copy(
            src_ref=acc.at[rows], dst_ref=other.at[rows], send_sem=swap_send.at[block], recv_sem=swap_sem.at[block],
            device_id=sibling, device_id_type=MESH)

    @pl.when(is_second)
    def _():
        prime(inverses, 1, 128, stage_wide)
        split_inverse(1, 0, 8)
        for block in range(4):
            part = x0.at[pl.ds(block * 256, 128)]
            pltpu.make_async_copy(part, part, direct_sem.at[block]).wait()
            for way in range(2):
                part = x0.at[pl.ds(block * 256 + 128 + way * 64, 64)]
                pltpu.make_async_copy(part, part, direct_sem.at[4 + block * 2 + way]).wait()
        spread_all(x0, w0, 1024)
        for block in range(4):
            rows, copy = swap(block)
            acc[rows, :] = product(first_low, block * 512, 512, w0)
            copy.start()

    relay_first_done = []

    @pl.when((row > 1))
    def _():
        prime(factor, 1, 256, stage)
        split_factor(1, second_low)

    relay(0, x0, holds0, True)

    @pl.when(is_second)
    def _():
        for block in range(4):
            rows, copy = swap(block)
            copy.wait_recv()

            def step(k, _):
                at_row = pl.multiple_of(block * 512 + k * 64, 64)
                here = pl.ds(at_row, 64)
                value = b[here, :] - (acc[here, :] + other[here, :])
                b[here, :] = value
                spread(value, wide, at_row, 64, 2048)
                return 0

            lax.fori_loop(0, 8, step, 0)
        for block in range(4):
            x1[pl.ds(block * 256, 256), :] = product(inverse_low, block * 256, 256, wide)

    for half in range(2):
        for index in range(SIDE):
            scatter(1, x1, half, index, holds1)
    relay(1, x1, holds1, True)

    collect(0, x0, holds0)
    solved0 = pltpu.make_async_copy(x0, solved_out.at[0], out_sem.at[0])
    solved0.start()

    @pl.when(row > 1)
    def _():
        spread_all(x0, w0, 1024)

        def step(block, _):
            at_row = pl.multiple_of(block * 512, 512)
            acc[pl.ds(at_row, 512), :] = product(first_low, at_row, 512, w0)
            return 0
        lax.fori_loop(0, 4, step, 0)

    collect(1, x1, holds1)
    solved1 = pltpu.make_async_copy(x1, solved_out.at[1], out_sem.at[1])
    solved1.start()

    mine = pl.multiple_of(col * 1024, 1024)
    theirs = pl.multiple_of((1 - col) * 1024, 1024)

    def swap_half(block):
        source = pl.ds(pl.multiple_of(theirs + block * 512, 512), 512)
        return pltpu.make_async_remote_copy(
            src_ref=acc.at[source], dst_ref=other.at[pl.ds(block * 512, 512)], send_sem=swap_send.at[block],
            recv_sem=swap_sem.at[block], device_id=sibling, device_id_type=MESH)

    @pl.when(row > 1)
    def _():
        spread_all(x1, w1, 1024)
        for block in range(2):
            here = pl.ds(pl.multiple_of(theirs + block * 512, 512), 512)
            acc[here, :] = acc[here, :] + product(second_low, theirs + block * 512, 512, w1)
            swap_half(block).start()
        for block in range(2):
            here = pl.ds(pl.multiple_of(mine + block * 512, 512), 512)
            acc[here, :] = acc[here, :] + product(second_low, mine + block * 512, 512, w1)
        for block in range(2):
            swap_half(block).wait_recv()
            here = pl.ds(pl.multiple_of(mine + block * 512, 512), 512)
            b[here, :] = b[here, :] - (acc[here, :] + other[pl.ds(block * 512, 512), :])
        for block in range(2):
            swap_half(block).wait_send()

    updated = pltpu.make_async_copy(b.at[pl.ds(mine, 1024)], updated_out, out_sem.at[2])
    updated.start()

    for condition, copy in pending:
        @pl.when(condition)
        def _():
            copy.wait_send()

    @pl.when(is_first)
    def _():
        for block in range(4):
            direct(block).wait_send()
            for way in range(2):
                aside(block, way).wait_send()

    @pl.when(is_detour)
    def _():
        for block in range(4):
            forward(block, 0).wait_send()

    @pl.when(is_second)
    def _():
        for block in range(4):
            swap(block)[1].wait_send()

    solved0.wait()
    solved1.wait()
    updated.wait()


def body(factor, inverses, rhs):
    dma = pltpu.SemaphoreType.DMA
    return pl.pallas_call(
        kernel,
        out_shape=(jax.ShapeDtypeStruct((2, 1024, LANES), F32), jax.ShapeDtypeStruct((1024, LANES), F32)),
        in_specs=[pl.BlockSpec(memory_space=pl.ANY)] * 3,
        out_specs=(pl.BlockSpec(memory_space=pl.ANY), pl.BlockSpec(memory_space=pl.ANY)),
        scratch_shapes=[
            pltpu.VMEM((2048, 2048), BF16),
            pltpu.VMEM((2048, 2048), BF16),
            pltpu.VMEM((1024, 4096), BF16),
            pltpu.VMEM((4, 256, 1024), F32),
            pltpu.VMEM((4, 128, 2048), F32),
            pltpu.VMEM((2048, LANES), F32),
            pltpu.VMEM((1024, LANES), F32),
            pltpu.VMEM((1024, LANES), F32),
            pltpu.VMEM((2048, 2 * LANES), BF16),
            pltpu.VMEM((2048, 2 * LANES), BF16),
            pltpu.VMEM((4096, 2 * LANES), BF16),
            pltpu.VMEM((2048, LANES), F32),
            pltpu.VMEM((2048, LANES), F32),
            pltpu.VMEM((256, LANES), F32),
            dma((4,)), dma, dma((2, 2, SIDE)), dma((2, 2, SIDE)), dma((2, 2, SIDE)), dma((2, 2, SIDE)),
            dma((12,)), dma((4,)), dma((4,)), dma((4, 2)), dma((4,)), dma((4,)), dma((4,)), dma((3,)),
        ],
        compiler_params=pltpu.CompilerParams(collective_id=0, has_side_effects=True, vmem_limit_bytes=56 * MIB),
        cost_estimate=pl.CostEstimate(flops=2 * 2 * 2048 * 1024 * 128, bytes_accessed=18 * MIB, transcendentals=0),
        name="block_steps",
    )(factor, inverses, rhs)


def solution(mesh):
    in_specs = (P(None, "row", "col"), P(None, "col", None), P("row", "rhs"))
    out_specs = (P(None, "col", "rhs"), P(("row", "col"), "rhs"))
    return jax.shard_map(body, mesh=mesh, in_specs=in_specs, out_specs=out_specs, check_vma=False)
```

time: 430 us -> 68.6 us (0.16)
  waiting for transfers between devices: 361 us -> 0 us
  Pallas kernels: 0 us -> 63.6 us
  matrix products: 48 us -> 0 us
  between operations: 13.8 us -> 0.64 us
    psum x3 -> x0, waiting for transfers between devices: 344 us -> none  [the longest x2 307 us: broadcast(): return lax.psum(block, axis)]
    pallas_call x0 -> x1, Pallas kernels: none -> 63.6 us  [body(): pl.pallas_call(kernel, out_shape=(jax.ShapeDtypeStruct((2, 1024, LANES),...]
    dot_general x4 -> x0, matrix products: 48 us -> none  [the longest x1 13.5 us: body(): jnp.dot(factor[1], second_solution, precision=precise, preferred_element_...]
    reduce_scatter x1 -> x0, waiting for transfers between devices: 16.7 us -> none  [body(): reduced = lax.psum_scatter(combined, 'col', scatter_dimension=0, tiled=True)]
  transfers between devices with their start and end apart: 4 -> 0, of which waited for: 4 -> 0; matrix products, arithmetic and copies ran while one was open for 1% -> 0% of each run, Pallas kernels for 0% -> 0%
where the time goes in v1:
time: 68.6 us; the launch traced here: 68.4 us
  Pallas kernels  63.6 us (93%)
  local copies, waits for them, and re-layouts  4.13 us (6%)
    pallas_call x1, Pallas kernels, body(): pl.pallas_call(kernel, out_shape=(jax.ShapeDtypeStruct((2, 1024, LANES),...  63.6 us
    unnamed x2, local copies, waits for them, and re-layouts  4.13 us

profile of v1, /device:TPU:57, one launch (start us, length us, event | category | flops | bytes accessed | tf_op | source)
XLA Modules:
  0.0 68.4 jit_solution(8745688467561159099)
XLA Ops:
  0.6 63.6 %block_steps.1 = (f32[2,1024,128]{2,1,0:T(8,128)}, f32[1024,128]{1,0:T(8,128)}) custom-call(f32[2,2048,1024]{2,1,0:T(8,128)} %factor.1, f32[2,1024,2048]{2,1,0:T(8,128)} %inverses.1, f32[2048,128]{1,0:T(8,128)} %rhs.1), custom_call_target="tpu_custom_call" | custom-call | flops 1073741824 | bytes 18874368 | tf_op jit(solution)/shard_map/block_steps/pallas_call | solution.py:368
  64.2 2.3 %copy.7 = f32[2,1024,128]{2,1,0:T(8,128)} copy(f32[2,1024,128]{2,1,0:T(8,128)} %get-tuple-element.4) | data formatting | bytes 2097152
  66.5 1.9 %copy.8 = f32[1024,128]{1,0:T(8,128)} copy(f32[1024,128]{1,0:T(8,128)} %get-tuple-element.5) | data formatting | bytes 1048576

commit v2 on v1

v2 whole, which is shorter than its diff:
```python
import functools

import jax
import jax.numpy as jnp
from jax import lax
from jax.experimental import pallas as pl
from jax.experimental.pallas import tpu as pltpu
from jax.sharding import PartitionSpec as P

MESH = pl.DeviceIdType.MESH
F32 = jnp.float32
BF16 = jnp.bfloat16
SIDE = 8
FAR_FIRST = (4, 3, 5, 2, 6, 1, 7)
HALF = 512
CHUNK = 256
LANES = 128
MIB = 1 << 20


def split(value):
    high = value.astype(BF16)
    return high, (value - high.astype(F32)).astype(BF16)


def kernel(
    factor, inverses, rhs, solved_out, updated_out,
    first_low, second_low, inverse_low, stage, stage_wide, b, x0, x1, w0, w1, wide, acc, other, detour,
    stage_sem, b_sem, piece_sem, scatter_sem, along_sem, across_sem, direct_sem, direct_send,
    detour_sem, detour_send, forward_send, swap_sem, swap_send, out_sem,
):
    row = lax.axis_index("row")
    col = lax.axis_index("col")
    y = lax.rem(row, SIDE)
    z = lax.div(row, SIDE)
    sibling = {"col": 1 - col}
    is_first = row == 0
    is_second = row == 1
    is_detour = (row == SIDE) | (row == 7 * SIDE)
    pending = []

    def load_factor(block):
        slot = lax.rem(block, 4)
        rows = pl.ds(pl.multiple_of(lax.rem(block, 8) * 256, 256), 256)
        return pltpu.make_async_copy(factor.at[lax.div(block, 8), rows], stage.at[slot], stage_sem.at[slot])

    def load_inverse(index, block):
        slot = lax.rem(block, 4)
        rows = pl.ds(pl.multiple_of(block * 128, 128), 128)
        return pltpu.make_async_copy(inverses.at[index, rows], stage_wide.at[slot], stage_sem.at[4 + slot])

    def split_rows(source, slot, rows, step_rows, target, base):
        chunks = source.shape[2] // CHUNK

        def part(k, _):
            at = pl.multiple_of(k * step_rows, step_rows)
            to = pl.ds(pl.multiple_of(base + at, step_rows), step_rows)
            for q in range(chunks):
                high, low = split(source[slot, pl.ds(at, step_rows), q * CHUNK:(q + 1) * CHUNK])
                target[to, 2 * q * CHUNK:(2 * q + 1) * CHUNK] = high
                target[to, (2 * q + 1) * CHUNK:(2 * q + 2) * CHUNK] = low
            return 0

        lax.fori_loop(0, rows // step_rows, part, 0)

    def split_factor(index, target, blocks):
        def step(k, _):
            block = index * 8 + k
            load_factor(block).wait()
            split_rows(stage, lax.rem(block, 4), 256, 64, target, k * 256)

            @pl.when(block + 4 < blocks)
            def _():
                load_factor(block + 4).start()
            return 0
        lax.fori_loop(0, 8, step, 0)

    def split_inverse(index, begin, count):
        def step(block, _):
            load_inverse(index, block).wait()
            split_rows(stage_wide, lax.rem(block, 4), 128, 32, inverse_low, block * 128)

            @pl.when(block + 4 < 8)
            def _():
                load_inverse(index, block + 4).start()
            return 0
        lax.fori_loop(begin, begin + count, step, 0)

    def spread(value, target, at):
        rows = value.shape[0]
        high, low = split(value)
        chunk, inside = lax.div(at, CHUNK), lax.rem(at, CHUNK)
        for part in range(2):
            to = pl.ds(pl.multiple_of(chunk * 2 * CHUNK + part * CHUNK + inside, 64), rows)
            target[to, :LANES] = high
            target[to, LANES:] = low

    def spread_rows(source, target, begin, count):
        def step(k, _):
            at = pl.multiple_of(begin + k * CHUNK, CHUNK)
            spread(source[pl.ds(at, CHUNK), :], target, at)
            return 0
        lax.fori_loop(0, count // CHUNK, step, 0)

    def product(matrix, at, rows, weights, first, count):
        columns = slice(2 * first * CHUNK, 2 * (first + count) * CHUNK)
        both = jnp.dot(matrix[pl.ds(pl.multiple_of(at, rows), rows), columns], weights[columns, :],
                       preferred_element_type=F32)
        return both[:, :LANES] + both[:, LANES:]

    b_copy = pltpu.make_async_copy(rhs, b, b_sem)
    b_copy.start()

    @pl.when(is_first | is_second)
    def _():
        for block in range(4):
            load_inverse(row, jnp.int32(block)).start()

    @pl.when(jnp.logical_not(is_first))
    def _():
        for block in range(4):
            load_factor(jnp.int32(block)).start()

    def at(yy, zz):
        return {"row": zz * SIDE + yy}

    barrier = pltpu.get_barrier_semaphore()
    for k in range(1, SIDE):
        pl.semaphore_signal(barrier, inc=1, device_id=at(lax.rem(y + k, SIDE), z), device_id_type=MESH)
        pl.semaphore_signal(barrier, inc=1, device_id=at(y, lax.rem(z + k, SIDE)), device_id_type=MESH)
    pl.semaphore_signal(barrier, inc=1, device_id=sibling, device_id_type=MESH)

    @pl.when(is_second)
    def _():
        for k in (1, 7):
            pl.semaphore_signal(barrier, inc=1, device_id={"row": k * SIDE}, device_id_type=MESH)

    def pass_barrier():
        @pl.when(is_detour)
        def _():
            pl.semaphore_wait(barrier, 16)

        @pl.when(jnp.logical_not(is_detour))
        def _():
            pl.semaphore_wait(barrier, 15)

    def layout(which, half):
        if which == 0 and half == 0:
            return 80, 32, 0, (0, 1)
        return 72, 8, (which if half == 0 else 0), ((which,) if half == 0 else (0,))

    def hub_rows(which, half, index):
        rows, _, owner, outside = layout(which, half)
        rank = index - len(outside) if owner == 0 else index - jnp.where(index > owner, 1, 0)
        return pl.ds(pl.multiple_of(half * HALF + rank * rows, 8), rows)

    def rest_rows(which, half):
        rest = layout(which, half)[1]
        return pl.ds((half + 1) * HALF - rest, rest)

    def is_hub(which, half, index):
        return functools.reduce(jnp.logical_and, [index != q for q in layout(which, half)[3]])

    def send(condition, buffer, rows, target, send_sem, recv_sem):
        copy = pltpu.make_async_remote_copy(
            src_ref=buffer.at[rows], dst_ref=buffer.at[rows], send_sem=send_sem, recv_sem=recv_sem,
            device_id=target, device_id_type=MESH,
        )

        @pl.when(condition)
        def _():
            copy.start()

        pending.append((condition, copy))

    def scatter(which, buffer, half, index):
        owner = which
        if index in layout(which, half)[3]:
            return
        place = index if half == 0 else index * SIDE + owner
        send(row == owner, buffer, hub_rows(which, half, jnp.int32(index)), {"row": place},
             scatter_sem.at[which, half, index], piece_sem.at[which, half, index])

    def among(place, holds):
        return functools.reduce(jnp.logical_or, [place == q for q in holds])

    def arrive(which, buffer, half, index, holds):
        outside = among(row, holds)

        def wait(rows):
            part = buffer.at[rows]
            pltpu.make_async_copy(part, part, piece_sem.at[which, half, index]).wait()

        @pl.when(jnp.logical_not(outside) & is_hub(which, half, index))
        def _():
            wait(hub_rows(which, half, index))

        @pl.when(jnp.logical_not(outside) & (index == layout(which, half)[2]))
        def _():
            wait(rest_rows(which, half))

    def relay(which, buffer, holds):
        for half in range(2):
            mine, cross, cross_owner = (y, z, 0) if half == 0 else (z, y, which)
            arrive(which, buffer, half, mine, holds)
            for step, sems in ((0, along_sem), (1, across_sem)):
                for k in FAR_FIRST:
                    if step == 0:
                        there = lax.rem(cross + k, SIDE)
                        target = y + there * SIDE if half == 0 else z * SIDE + there
                    else:
                        there = lax.rem(mine + k, SIDE)
                        target = z * SIDE + there if half == 0 else y + there * SIDE
                    go = jnp.logical_not(among(target, holds))
                    if step == 0:
                        go = go & (cross == cross_owner)
                    send(go & is_hub(which, half, mine), buffer, hub_rows(which, half, mine), {"row": target},
                         sems.at[which, half, k], piece_sem.at[which, half, mine])
                    send(go & (mine == layout(which, half)[2]), buffer, rest_rows(which, half), {"row": target},
                         sems.at[which, half, k], piece_sem.at[which, half, mine])

    def collect(which, buffer, half, holds):
        for k in (1, 7, 2, 6, 3, 5, 4):
            arrive(which, buffer, half, lax.rem((y if half == 0 else z) + k, SIDE), holds)

    holds0, holds1 = (0, 1), (1,)

    def direct(block):
        return pltpu.make_async_remote_copy(
            src_ref=x0.at[pl.ds(block * 256, 128)], dst_ref=x0.at[pl.ds(block * 256, 128)],
            send_sem=direct_send.at[block], recv_sem=direct_sem.at[block], device_id={"row": 1}, device_id_type=MESH)

    def aside(block, way):
        return pltpu.make_async_remote_copy(
            src_ref=x0.at[pl.ds(block * 256 + 128 + way * 64, 64)], dst_ref=detour.at[pl.ds(block * 64, 64)],
            send_sem=detour_send.at[block, way], recv_sem=detour_sem.at[block],
            device_id={"row": (SIDE, 7 * SIDE)[way]}, device_id_type=MESH)

    def forward(block, way):
        return pltpu.make_async_remote_copy(
            src_ref=detour.at[pl.ds(block * 64, 64)], dst_ref=x0.at[pl.ds(block * 256 + 128 + way * 64, 64)],
            send_sem=forward_send.at[block], recv_sem=direct_sem.at[4 + block * 2 + way],
            device_id={"row": 1}, device_id_type=MESH)

    @pl.when(is_first)
    def _():
        b_copy.wait()
        spread_rows(b, wide, 0, 2048)
        for block in range(4):
            split_inverse(0, 2 * block, 2)
            x0[pl.ds(block * 256, 256), :] = product(inverse_low, block * 256, 256, wide, 0, 8)
            if block == 0:
                pass_barrier()
            direct(block).start()
            for way in range(2):
                aside(block, way).start()

    @pl.when(jnp.logical_not(is_first))
    def _():
        b_copy.wait()
        split_factor(0, first_low, jnp.where(is_second, 8, 16))
        pass_barrier()

    for index in (5, 6, 7):
        scatter(0, x0, 0, index)
    for index in (4, 3, 5, 2, 6, 1, 7):
        scatter(0, x0, 1, index)
    for index in (4, 3, 2):
        scatter(0, x0, 0, index)

    for way in range(2):
        @pl.when(row == (SIDE, 7 * SIDE)[way])
        def _():
            for block in range(4):
                part = detour.at[pl.ds(block * 64, 64)]
                pltpu.make_async_copy(part, part, detour_sem.at[block]).wait()
                forward(block, way).start()

    def swap(block):
        rows = pl.ds(pl.multiple_of(block * 512, 512), 512)
        return rows, pltpu.make_async_remote_copy(
            src_ref=acc.at[rows], dst_ref=other.at[rows], send_sem=swap_send.at[block], recv_sem=swap_sem.at[block],
            device_id=sibling, device_id_type=MESH)

    @pl.when(is_second)
    def _():
        split_inverse(1, 0, 8)
        for chunk in range(4):
            part = x0.at[pl.ds(chunk * 256, 128)]
            pltpu.make_async_copy(part, part, direct_sem.at[chunk]).wait()
            for way in range(2):
                part = x0.at[pl.ds(chunk * 256 + 128 + way * 64, 64)]
                pltpu.make_async_copy(part, part, direct_sem.at[4 + chunk * 2 + way]).wait()
            spread_rows(x0, w0, chunk * CHUNK, CHUNK)
            for block in range(4):
                rows, copy = swap(block)
                term = product(first_low, block * 512, 512, w0, chunk, 1)
                acc[rows, :] = term if chunk == 0 else acc[rows, :] + term
                if chunk == 3:
                    copy.start()

    @pl.when(row > 1)
    def _():
        split_factor(1, second_low, 16)

    relay(0, x0, holds0)

    @pl.when(is_second)
    def _():
        for block in range(4):
            rows, copy = swap(block)
            copy.wait_recv()
            for part in range(2):
                here = pl.ds(block * 512 + part * CHUNK, CHUNK)
                value = b[here, :] - (acc[here, :] + other[here, :])
                b[here, :] = value
                spread(value, wide, jnp.int32(block * 512 + part * CHUNK))
            for part in range(2):
                here = pl.ds(part * 512, 512)
                term = product(inverse_low, part * 512, 512, wide, 2 * block, 2)
                x1[here, :] = term if block == 0 else x1[here, :] + term

    for index in (5, 4, 6, 3, 7, 0, 2):
        scatter(1, x1, 0, index)
        scatter(1, x1, 1, (index + 7) % SIDE)
    relay(1, x1, holds1)

    collect(0, x0, 0, holds0)
    collect(0, x0, 1, holds0)
    solved0 = pltpu.make_async_copy(x0, solved_out.at[0], out_sem.at[0])
    solved0.start()

    @pl.when(row > 1)
    def _():
        spread_rows(x0, w0, 0, 1024)

        def step(block, _):
            at_row = pl.multiple_of(block * 512, 512)
            acc[pl.ds(at_row, 512), :] = product(first_low, at_row, 512, w0, 0, 4)
            return 0
        lax.fori_loop(0, 4, step, 0)

    collect(1, x1, 0, holds1)

    @pl.when(row > 1)
    def _():
        spread_rows(x1, w1, 0, 512)

        def step(block, _):
            at_row = pl.multiple_of(block * 512, 512)
            rows = pl.ds(at_row, 512)
            acc[rows, :] = acc[rows, :] + product(second_low, at_row, 512, w1, 0, 2)
            return 0
        lax.fori_loop(0, 4, step, 0)

    collect(1, x1, 1, holds1)
    solved1 = pltpu.make_async_copy(x1, solved_out.at[1], out_sem.at[1])
    solved1.start()

    mine = pl.multiple_of(col * 1024, 1024)
    theirs = pl.multiple_of((1 - col) * 1024, 1024)

    def swap_half(block):
        source = pl.ds(pl.multiple_of(theirs + block * 512, 512), 512)
        return pltpu.make_async_remote_copy(
            src_ref=acc.at[source], dst_ref=other.at[pl.ds(block * 512, 512)], send_sem=swap_send.at[block],
            recv_sem=swap_sem.at[block], device_id=sibling, device_id_type=MESH)

    @pl.when(row > 1)
    def _():
        spread_rows(x1, w1, 512, 512)
        for block in range(2):
            here = pl.ds(pl.multiple_of(theirs + block * 512, 512), 512)
            acc[here, :] = acc[here, :] + product(second_low, theirs + block * 512, 512, w1, 2, 2)
            swap_half(block).start()
        for block in range(2):
            here = pl.ds(pl.multiple_of(mine + block * 512, 512), 512)
            b[here, :] = b[here, :] - (acc[here, :] + product(second_low, mine + block * 512, 512, w1, 2, 2))
        for block in range(2):
            swap_half(block).wait_recv()
            here = pl.ds(pl.multiple_of(mine + block * 512, 512), 512)
            b[here, :] = b[here, :] - other[pl.ds(block * 512, 512), :]
        for block in range(2):
            swap_half(block).wait_send()

    updated = pltpu.make_async_copy(b.at[pl.ds(mine, 1024)], updated_out, out_sem.at[2])
    updated.start()

    for condition, copy in pending:
        @pl.when(condition)
        def _():
            copy.wait_send()

    @pl.when(is_first)
    def _():
        for block in range(4):
            direct(block).wait_send()
            for way in range(2):
                aside(block, way).wait_send()

    @pl.when(is_detour)
    def _():
        for block in range(4):
            forward(block, 0).wait_send()

    @pl.when(is_second)
    def _():
        for block in range(4):
            swap(block)[1].wait_send()

    solved0.wait()
    solved1.wait()
    updated.wait()


def body(factor, inverses, rhs):
    dma = pltpu.SemaphoreType.DMA
    return pl.pallas_call(
        kernel,
        out_shape=(jax.ShapeDtypeStruct((2, 1024, LANES), F32), jax.ShapeDtypeStruct((1024, LANES), F32)),
        in_specs=[pl.BlockSpec(memory_space=pl.ANY)] * 3,
        out_specs=(pl.BlockSpec(memory_space=pl.ANY), pl.BlockSpec(memory_space=pl.ANY)),
        scratch_shapes=[
            pltpu.VMEM((2048, 2048), BF16),
            pltpu.VMEM((2048, 2048), BF16),
            pltpu.VMEM((1024, 4096), BF16),
            pltpu.VMEM((4, 256, 1024), F32),
            pltpu.VMEM((4, 128, 2048), F32),
            pltpu.VMEM((2048, LANES), F32),
            pltpu.VMEM((1024, LANES), F32),
            pltpu.VMEM((1024, LANES), F32),
            pltpu.VMEM((2048, 2 * LANES), BF16),
            pltpu.VMEM((2048, 2 * LANES), BF16),
            pltpu.VMEM((4096, 2 * LANES), BF16),
            pltpu.VMEM((2048, LANES), F32),
            pltpu.VMEM((2048, LANES), F32),
            pltpu.VMEM((256, LANES), F32),
            dma((8,)), dma, dma((2, 2, SIDE)), dma((2, 2, SIDE)), dma((2, 2, SIDE)), dma((2, 2, SIDE)),
            dma((12,)), dma((4,)), dma((4,)), dma((4, 2)), dma((4,)), dma((4,)), dma((4,)), dma((3,)),
        ],
        compiler_params=pltpu.CompilerParams(collective_id=0, has_side_effects=True, vmem_limit_bytes=56 * MIB),
        cost_estimate=pl.CostEstimate(flops=2 * 2 * 2048 * 1024 * 128, bytes_accessed=18 * MIB, transcendentals=0),
        name="block_steps",
    )(factor, inverses, rhs)


def solution(mesh):
    in_specs = (P(None, "row", "col"), P(None, "col", None), P("row", "rhs"))
    out_specs = (P(None, "col", "rhs"), P(("row", "col"), "rhs"))
    return jax.shard_map(body, mesh=mesh, in_specs=in_specs, out_specs=out_specs, check_vma=False)
```

time: 68.6 us -> 59.7 us (0.87)
  Pallas kernels: 63.6 us -> 54.7 us
    pallas_call x1, Pallas kernels: 63.6 us -> 54.7 us  [body(): pl.pallas_call(kernel, out_shape=(jax.ShapeDtypeStruct((2, 1024, LANES),...]
where the time goes in v2:
time: 59.7 us; the launch traced here: 59.5 us
  Pallas kernels  54.7 us (92%)
  local copies, waits for them, and re-layouts  4.13 us (7%)
  between operations  0.64 us (1%)
    pallas_call x1, Pallas kernels, body(): pl.pallas_call(kernel, out_shape=(jax.ShapeDtypeStruct((2, 1024, LANES),...  54.7 us
    unnamed x2, local copies, waits for them, and re-layouts  4.13 us

profile of v2, /device:TPU:57, one launch (start us, length us, event | category | flops | bytes accessed | tf_op | source)
XLA Modules:
  0.0 59.5 jit_solution(15256797037813982768)
XLA Ops:
  0.6 54.7 %block_steps.1 = (f32[2,1024,128]{2,1,0:T(8,128)}, f32[1024,128]{1,0:T(8,128)}) custom-call(f32[2,2048,1024]{2,1,0:T(8,128)} %factor.1, f32[2,1024,2048]{2,1,0:T(8,128)} %inverses.1, f32[2048,128]{1,0:T(8,128)} %rhs.1), custom_call_target="tpu_custom_call" | custom-call | flops 1073741824 | bytes 18874368 | tf_op jit(solution)/shard_map/block_steps/pallas_call | solution.py:418
  55.3 2.3 %copy.7 = f32[2,1024,128]{2,1,0:T(8,128)} copy(f32[2,1024,128]{2,1,0:T(8,128)} %get-tuple-element.4) | data formatting | bytes 2097152
  57.6 1.9 %copy.8 = f32[1024,128]{1,0:T(8,128)} copy(f32[1024,128]{1,0:T(8,128)} %get-tuple-element.5) | data formatting | bytes 1048576

commit v3 on v2

--- a/solution.py
+++ b/solution.py
@@ -45,9 +45,8 @@
         return pltpu.make_async_copy(factor.at[lax.div(block, 8), rows], stage.at[slot], stage_sem.at[slot])
 
     def load_inverse(index, block):
-        slot = lax.rem(block, 4)
-        rows = pl.ds(pl.multiple_of(block * 128, 128), 128)
-        return pltpu.make_async_copy(inverses.at[index, rows], stage_wide.at[slot], stage_sem.at[4 + slot])
+        rows = pl.ds(pl.multiple_of(block * 256, 256), 256)
+        return pltpu.make_async_copy(inverses.at[index, rows], stage_wide.at[block], stage_sem.at[4 + block])
 
     def split_rows(source, slot, rows, step_rows, target, base):
         chunks = source.shape[2] // CHUNK
@@ -75,16 +74,12 @@
             return 0
         lax.fori_loop(0, 8, step, 0)
 
-    def split_inverse(index, begin, count):
+    def split_inverse(index):
         def step(block, _):
             load_inverse(index, block).wait()
-            split_rows(stage_wide, lax.rem(block, 4), 128, 32, inverse_low, block * 128)
-
-            @pl.when(block + 4 < 8)
-            def _():
-                load_inverse(index, block + 4).start()
-            return 0
-        lax.fori_loop(begin, begin + count, step, 0)
+            split_rows(stage_wide, block, 256, 32, inverse_low, block * 256)
+            return 0
+        lax.fori_loop(0, 4, step, 0)
 
     def spread(value, target, at):
         rows = value.shape[0]
@@ -106,6 +101,15 @@
         columns = slice(2 * first * CHUNK, 2 * (first + count) * CHUNK)
         both = jnp.dot(matrix[pl.ds(pl.multiple_of(at, rows), rows), columns], weights[columns, :],
                        preferred_element_type=F32)
+        return both[:, :LANES] + both[:, LANES:]
+
+    def split_product(source, slot, weights):
+        total = None
+        for q in range(source.shape[2] // CHUNK):
+            parts = jnp.concatenate(split(source[slot, :, q * CHUNK:(q + 1) * CHUNK]), axis=0)
+            term = jnp.dot(parts, weights[2 * q * CHUNK:(2 * q + 1) * CHUNK, :], preferred_element_type=F32)
+            total = term if total is None else total + term
+        both = total[:256, :] + total[256:, :]
         return both[:, :LANES] + both[:, LANES:]
 
     b_copy = pltpu.make_async_copy(rhs, b, b_sem)
@@ -247,8 +251,8 @@
         b_copy.wait()
         spread_rows(b, wide, 0, 2048)
         for block in range(4):
-            split_inverse(0, 2 * block, 2)
-            x0[pl.ds(block * 256, 256), :] = product(inverse_low, block * 256, 256, wide, 0, 8)
+            load_inverse(0, jnp.int32(block)).wait()
+            x0[pl.ds(block * 256, 256), :] = split_product(stage_wide, block, wide)
             if block == 0:
                 pass_barrier()
             direct(block).start()
@@ -284,7 +288,7 @@
 
     @pl.when(is_second)
     def _():
-        split_inverse(1, 0, 8)
+        split_inverse(1)
         for chunk in range(4):
             part = x0.at[pl.ds(chunk * 256, 128)]
             pltpu.make_async_copy(part, part, direct_sem.at[chunk]).wait()
@@ -418,14 +422,14 @@
     return pl.pallas_call(
         kernel,
         out_shape=(jax.ShapeDtypeStruct((2, 1024, LANES), F32), jax.ShapeDtypeStruct((1024, LANES), F32)),
-        in_specs=[pl.BlockSpec(memory_space=pl.ANY)] * 3,
+        in_specs=[pl.BlockSpec(memory_space=pltpu.HBM)] * 3,
         out_specs=(pl.BlockSpec(memory_space=pl.ANY), pl.BlockSpec(memory_space=pl.ANY)),
         scratch_shapes=[
             pltpu.VMEM((2048, 2048), BF16),
             pltpu.VMEM((2048, 2048), BF16),
             pltpu.VMEM((1024, 4096), BF16),
             pltpu.VMEM((4, 256, 1024), F32),
-            pltpu.VMEM((4, 128, 2048), F32),
+            pltpu.VMEM((4, 256, 2048), F32),
             pltpu.VMEM((2048, LANES), F32),
             pltpu.VMEM((1024, LANES), F32),
             pltpu.VMEM((1024, LANES), F32),
@@ -438,7 +442,7 @@
             dma((8,)), dma, dma((2, 2, SIDE)), dma((2, 2, SIDE)), dma((2, 2, SIDE)), dma((2, 2, SIDE)),
             dma((12,)), dma((4,)), dma((4,)), dma((4, 2)), dma((4,)), dma((4,)), dma((4,)), dma((3,)),
         ],
-        compiler_params=pltpu.CompilerParams(collective_id=0, has_side_effects=True, vmem_limit_bytes=56 * MIB),
+        compiler_params=pltpu.CompilerParams(collective_id=0, has_side_effects=True, vmem_limit_bytes=48 * MIB),
         cost_estimate=pl.CostEstimate(flops=2 * 2 * 2048 * 1024 * 128, bytes_accessed=18 * MIB, transcendentals=0),
         name="block_steps",
     )(factor, inverses, rhs)

time: 59.7 us -> 59.1 us (0.990)
  local copies, waits for them, and re-layouts: 4.13 us -> 2.98 us
    unnamed x2 -> x4, local copies, waits for them, and re-layouts: 4.13 us -> 2.98 us
where the time goes in v3:
time: 59.1 us; the launch traced here: 58.5 us
  Pallas kernels  54.9 us (93%)
  local copies, waits for them, and re-layouts  2.98 us (5%)
  between operations  0.65 us (1%)
    pallas_call x1, Pallas kernels, body(): pl.pallas_call(kernel, out_shape=(jax.ShapeDtypeStruct((2, 1024, LANES),...  54.9 us
    unnamed x4, local copies, waits for them, and re-layouts  2.98 us

profile of v3, /device:TPU:57, one launch (start us, length us, event | category | flops | bytes accessed | tf_op | source)
XLA Modules:
  0.0 58.5 jit_solution(9179264996224930598)
XLA Ops:
  0.6 0.0 copy-start
  0.6 1.2 %copy-done = f32[2048,128]{1,0:T(8,128)S(1)} copy-done((f32[2048,128]{1,0:T(8,128)S(1)}, f32[2048,128]{1,0:T(8,128)}, u32[]{:S(2)}) %copy-start) | copy-done | bytes 1048600
  1.9 54.9 %block_steps.1 = (f32[2,1024,128]{2,1,0:T(8,128)S(1)}, f32[1024,128]{1,0:T(8,128)S(1)}) custom-call(f32[2,2048,1024]{2,1,0:T(8,128)} %factor.1, f32[2,1024,2048]{2,1,0:T(8,128)} %inverses.1, f32[2048,128]{1,0:T(8,128)S(1)} %copy-done), custom_call_target="tpu_custom_call" | custom-call | flops 1073741824 | bytes 18874368 | tf_op jit(solution)/shard_map/block_steps/pallas_call | solution.py:422
  56.7 1.0 %copy.7 = f32[2,1024,128]{2,1,0:T(8,128)} copy(f32[2,1024,128]{2,1,0:T(8,128)S(1)} %get-tuple-element.4) | data formatting | bytes 2097152
  57.7 0.8 %copy.8 = f32[1024,128]{1,0:T(8,128)} copy(f32[1024,128]{1,0:T(8,128)S(1)} %get-tuple-element.5) | data formatting | bytes 1048576
Async XLA Ops:
  0.6 1.2 %copy-start = (f32[2048,128]{1,0:T(8,128)S(1)}, f32[2048,128]{1,0:T(8,128)}, u32[]{:S(2)}) copy-start(f32[2048,128]{1,0:T(8,128)} %rhs.1) | copy-start | bytes 3145732

commit v4 on v3

--- a/solution.py
+++ b/solution.py
@@ -27,7 +27,7 @@
     factor, inverses, rhs, solved_out, updated_out,
     first_low, second_low, inverse_low, stage, stage_wide, b, x0, x1, w0, w1, wide, acc, other, detour,
     stage_sem, b_sem, piece_sem, scatter_sem, along_sem, across_sem, direct_sem, direct_send,
-    detour_sem, detour_send, forward_send, swap_sem, swap_send, out_sem,
+    detour_sem, detour_send, forward_send, swap_sem, swap_send, out_sem, last_sem,
 ):
     row = lax.axis_index("row")
     col = lax.axis_index("col")
@@ -39,6 +39,20 @@
     is_detour = (row == SIDE) | (row == 7 * SIDE)
     pending = []
 
+    def at(yy, zz):
+        return {"row": zz * SIDE + yy}
+
+    barrier = pltpu.get_barrier_semaphore()
+    for k in FAR_FIRST:
+        pl.semaphore_signal(barrier, inc=1, device_id=at(lax.rem(y + k, SIDE), z), device_id_type=MESH)
+        pl.semaphore_signal(barrier, inc=1, device_id=at(y, lax.rem(z + k, SIDE)), device_id_type=MESH)
+    pl.semaphore_signal(barrier, inc=1, device_id=sibling, device_id_type=MESH)
+
+    @pl.when(is_second)
+    def _():
+        for k in (1, 7):
+            pl.semaphore_signal(barrier, inc=1, device_id={"row": k * SIDE}, device_id_type=MESH)
+
     def load_factor(block):
         slot = lax.rem(block, 4)
         rows = pl.ds(pl.multiple_of(lax.rem(block, 8) * 256, 256), 256)
@@ -125,20 +139,6 @@
         for block in range(4):
             load_factor(jnp.int32(block)).start()
 
-    def at(yy, zz):
-        return {"row": zz * SIDE + yy}
-
-    barrier = pltpu.get_barrier_semaphore()
-    for k in range(1, SIDE):
-        pl.semaphore_signal(barrier, inc=1, device_id=at(lax.rem(y + k, SIDE), z), device_id_type=MESH)
-        pl.semaphore_signal(barrier, inc=1, device_id=at(y, lax.rem(z + k, SIDE)), device_id_type=MESH)
-    pl.semaphore_signal(barrier, inc=1, device_id=sibling, device_id_type=MESH)
-
-    @pl.when(is_second)
-    def _():
-        for k in (1, 7):
-            pl.semaphore_signal(barrier, inc=1, device_id={"row": k * SIDE}, device_id_type=MESH)
-
     def pass_barrier():
         @pl.when(is_detour)
         def _():
@@ -209,6 +209,8 @@
             arrive(which, buffer, half, mine, holds)
             for step, sems in ((0, along_sem), (1, across_sem)):
                 for k in FAR_FIRST:
+                    if step == 1 and which == 0 and k == 4:
+                        continue
                     if step == 0:
                         there = lax.rem(cross + k, SIDE)
                         target = y + there * SIDE if half == 0 else z * SIDE + there
@@ -223,8 +225,20 @@
                     send(go & (mine == layout(which, half)[2]), buffer, rest_rows(which, half), {"row": target},
                          sems.at[which, half, k], piece_sem.at[which, half, mine])
 
+    def last_hop(which, buffer, holds):
+        for half in range(2):
+            mine = y if half == 0 else z
+            source, there = lax.rem(mine + 3, SIDE), lax.rem(mine + 7, SIDE)
+            arrive(which, buffer, half, source, holds)
+            target = z * SIDE + there if half == 0 else y + there * SIDE
+            go = jnp.logical_not(among(target, holds))
+            send(go & is_hub(which, half, source), buffer, hub_rows(which, half, source), {"row": target},
+                 last_sem.at[half], piece_sem.at[which, half, source])
+            send(go & (source == layout(which, half)[2]), buffer, rest_rows(which, half), {"row": target},
+                 last_sem.at[half], piece_sem.at[which, half, source])
+
     def collect(which, buffer, half, holds):
-        for k in (1, 7, 2, 6, 3, 5, 4):
+        for k in (1, 7, 2, 6, 5, 4) if which == 0 else (1, 7, 2, 6, 3, 5, 4):
             arrive(which, buffer, half, lax.rem((y if half == 0 else z) + k, SIDE), holds)
 
     holds0, holds1 = (0, 1), (1,)
@@ -327,6 +341,7 @@
     for index in (5, 4, 6, 3, 7, 0, 2):
         scatter(1, x1, 0, index)
         scatter(1, x1, 1, (index + 7) % SIDE)
+    last_hop(0, x0, holds0)
     relay(1, x1, holds1)
 
     collect(0, x0, 0, holds0)
@@ -440,9 +455,9 @@
             pltpu.VMEM((2048, LANES), F32),
             pltpu.VMEM((256, LANES), F32),
             dma((8,)), dma, dma((2, 2, SIDE)), dma((2, 2, SIDE)), dma((2, 2, SIDE)), dma((2, 2, SIDE)),
-            dma((12,)), dma((4,)), dma((4,)), dma((4, 2)), dma((4,)), dma((4,)), dma((4,)), dma((3,)),
+            dma((12,)), dma((4,)), dma((4,)), dma((4, 2)), dma((4,)), dma((4,)), dma((4,)), dma((3,)), dma((2,)),
         ],
-        compiler_params=pltpu.CompilerParams(collective_id=0, has_side_effects=True, vmem_limit_bytes=48 * MIB),
+        compiler_params=pltpu.CompilerParams(collective_id=0, has_side_effects=True, vmem_limit_bytes=52 * MIB),
         cost_estimate=pl.CostEstimate(flops=2 * 2 * 2048 * 1024 * 128, bytes_accessed=18 * MIB, transcendentals=0),
         name="block_steps",
     )(factor, inverses, rhs)

time: 59.1 us -> 58.3 us (0.986)
  local copies, waits for them, and re-layouts: 2.98 us -> 1.77 us
  Pallas kernels: 54.9 us -> 55.6 us
    unnamed x4 -> x2, local copies, waits for them, and re-layouts: 2.98 us -> 1.77 us
    pallas_call x1, Pallas kernels: 54.9 us -> 55.6 us  [body(): pl.pallas_call(kernel, out_shape=(jax.ShapeDtypeStruct((2, 1024, LANES),...]
where the time goes in v4:
time: 58.3 us; the launch traced here: 58 us
  Pallas kernels  55.6 us (95%)
  local copies, waits for them, and re-layouts  1.77 us (3%)
  between operations  0.64 us (1%)
    pallas_call x1, Pallas kernels, body(): pl.pallas_call(kernel, out_shape=(jax.ShapeDtypeStruct((2, 1024, LANES),...  55.6 us
    unnamed x2, local copies, waits for them, and re-layouts  1.77 us

profile of v4, /device:TPU:57, one launch (start us, length us, event | category | flops | bytes accessed | tf_op | source)
XLA Modules:
  0.0 58.0 jit_solution(12867691217199476026)
XLA Ops:
  0.6 55.6 %block_steps.1 = (f32[2,1024,128]{2,1,0:T(8,128)S(1)}, f32[1024,128]{1,0:T(8,128)S(1)}) custom-call(f32[2,2048,1024]{2,1,0:T(8,128)} %factor.1, f32[2,1024,2048]{2,1,0:T(8,128)} %inverses.1, f32[2048,128]{1,0:T(8,128)} %rhs.1), custom_call_target="tpu_custom_call" | custom-call | flops 1073741824 | bytes 18874368 | tf_op jit(solution)/shard_map/block_steps/pallas_call | solution.py:437
  56.3 1.0 %copy.7 = f32[2,1024,128]{2,1,0:T(8,128)} copy(f32[2,1024,128]{2,1,0:T(8,128)S(1)} %get-tuple-element.4) | data formatting | bytes 2097152
  57.3 0.8 %copy.8 = f32[1024,128]{1,0:T(8,128)} copy(f32[1024,128]{1,0:T(8,128)S(1)} %get-tuple-element.5) | data formatting | bytes 1048576

commit v5 on v4

--- a/solution.py
+++ b/solution.py
@@ -432,9 +432,18 @@
     updated.wait()
 
 
+def write_out(solved, updated, solved_out, updated_out, sem):
+    copies = [pltpu.make_async_copy(solved.at[k], solved_out.at[k], sem.at[k]) for k in range(2)]
+    copies.append(pltpu.make_async_copy(updated, updated_out, sem.at[2]))
+    for copy in copies:
+        copy.start()
+    for copy in copies:
+        copy.wait()
+
+
 def body(factor, inverses, rhs):
     dma = pltpu.SemaphoreType.DMA
-    return pl.pallas_call(
+    results = pl.pallas_call(
         kernel,
         out_shape=(jax.ShapeDtypeStruct((2, 1024, LANES), F32), jax.ShapeDtypeStruct((1024, LANES), F32)),
         in_specs=[pl.BlockSpec(memory_space=pltpu.HBM)] * 3,
@@ -461,6 +470,16 @@
         cost_estimate=pl.CostEstimate(flops=2 * 2 * 2048 * 1024 * 128, bytes_accessed=18 * MIB, transcendentals=0),
         name="block_steps",
     )(factor, inverses, rhs)
+    return pl.pallas_call(
+        write_out,
+        out_shape=tuple(jax.ShapeDtypeStruct(r.shape, r.dtype) for r in results),
+        in_specs=[pl.BlockSpec(memory_space=pl.ANY)] * 2,
+        out_specs=(pl.BlockSpec(memory_space=pl.ANY), pl.BlockSpec(memory_space=pl.ANY)),
+        scratch_shapes=[dma((3,))],
+        compiler_params=pltpu.CompilerParams(vmem_limit_bytes=MIB),
+        cost_estimate=pl.CostEstimate(flops=0, bytes_accessed=3 * MIB, transcendentals=0),
+        name="write_out",
+    )(*results)
 
 
 def solution(mesh):

time: 58.3 us -> 57.7 us (0.990)
  local copies, waits for them, and re-layouts: 1.77 us -> 0 us
  Pallas kernels: 55.6 us -> 56.8 us
    unnamed x2 -> x0, local copies, waits for them, and re-layouts: 1.77 us -> none
    pallas_call x0 -> x1, Pallas kernels: none -> 1.17 us  [body(): pl.pallas_call(write_out, out_shape=tuple((jax.ShapeDtypeStruct(r.shape,...]
where the time goes in v5:
time: 57.7 us; the launch traced here: 57.4 us
  Pallas kernels  56.8 us (98%)
  between operations  0.64 us (1%)
    pallas_call x1, Pallas kernels, body(): pl.pallas_call(kernel, out_shape=(jax.ShapeDtypeStruct((2, 1024, LANES),...  55.6 us
    pallas_call x1, Pallas kernels, body(): pl.pallas_call(write_out, out_shape=tuple((jax.ShapeDtypeStruct(r.shape,...  1.17 us

profile of v5, /device:TPU:57, one launch (start us, length us, event | category | flops | bytes accessed | tf_op | source)
XLA Modules:
  0.0 57.4 jit_solution(18291931190445170556)
XLA Ops:
  0.6 55.6 %block_steps.1 = (f32[2,1024,128]{2,1,0:T(8,128)S(1)}, f32[1024,128]{1,0:T(8,128)S(1)}) custom-call(f32[2,2048,1024]{2,1,0:T(8,128)} %factor.1, f32[2,1024,2048]{2,1,0:T(8,128)} %inverses.1, f32[2048,128]{1,0:T(8,128)} %rhs.1), custom_call_target="tpu_custom_call" | custom-call | flops 1073741824 | bytes 18874368 | tf_op jit(solution)/shard_map/block_steps/pallas_call | solution.py:446
  56.3 1.2 %write_out.1 = (f32[2,1024,128]{2,1,0:T(8,128)}, f32[1024,128]{1,0:T(8,128)}) custom-call(f32[2,1024,128]{2,1,0:T(8,128)S(1)} %get-tuple-element.4.solved, f32[1024,128]{1,0:T(8,128)S(1)} %get-tuple-element.5.updated), custom_call_target="tpu_custom_call" | custom-call | bytes 3145728 | tf_op jit(solution)/shard_map/write_out/pallas_call | solution.py:473

commit v6 on v5

--- a/solution.py
+++ b/solution.py
@@ -27,7 +27,7 @@
     factor, inverses, rhs, solved_out, updated_out,
     first_low, second_low, inverse_low, stage, stage_wide, b, x0, x1, w0, w1, wide, acc, other, detour,
     stage_sem, b_sem, piece_sem, scatter_sem, along_sem, across_sem, direct_sem, direct_send,
-    detour_sem, detour_send, forward_send, swap_sem, swap_send, out_sem, last_sem,
+    detour_sem, detour_send, forward_send, swap_sem, swap_send, out_sem, last_sem, ready_sem,
 ):
     row = lax.axis_index("row")
     col = lax.axis_index("col")
@@ -43,10 +43,19 @@
         return {"row": zz * SIDE + yy}
 
     barrier = pltpu.get_barrier_semaphore()
+
+    def greet(target):
+        @pl.when((target["row"] != 0) | is_second | is_detour)
+        def _():
+            pl.semaphore_signal(barrier, inc=1, device_id=target, device_id_type=MESH)
+
     for k in FAR_FIRST:
-        pl.semaphore_signal(barrier, inc=1, device_id=at(lax.rem(y + k, SIDE), z), device_id_type=MESH)
-        pl.semaphore_signal(barrier, inc=1, device_id=at(y, lax.rem(z + k, SIDE)), device_id_type=MESH)
-    pl.semaphore_signal(barrier, inc=1, device_id=sibling, device_id_type=MESH)
+        greet(at(lax.rem(y + k, SIDE), z))
+        greet(at(y, lax.rem(z + k, SIDE)))
+
+    @pl.when(jnp.logical_not(is_first))
+    def _():
+        pl.semaphore_signal(barrier, inc=1, device_id=sibling, device_id_type=MESH)
 
     @pl.when(is_second)
     def _():
@@ -144,9 +153,13 @@
         def _():
             pl.semaphore_wait(barrier, 16)
 
-        @pl.when(jnp.logical_not(is_detour))
+        @pl.when(jnp.logical_not(is_detour | is_first))
         def _():
             pl.semaphore_wait(barrier, 15)
+
+        @pl.when(jnp.logical_not(is_detour | is_second) & ((y == 0) != (z == 0)))
+        def _():
+            pl.semaphore_signal(ready_sem, inc=1, device_id={"row": 0}, device_id_type=MESH)
 
     def layout(which, half):
         if which == 0 and half == 0:
@@ -268,7 +281,7 @@
             load_inverse(0, jnp.int32(block)).wait()
             x0[pl.ds(block * 256, 256), :] = split_product(stage_wide, block, wide)
             if block == 0:
-                pass_barrier()
+                pl.semaphore_wait(barrier, 3)
             direct(block).start()
             for way in range(2):
                 aside(block, way).start()
@@ -278,6 +291,10 @@
         b_copy.wait()
         split_factor(0, first_low, jnp.where(is_second, 8, 16))
         pass_barrier()
+
+    @pl.when(is_first)
+    def _():
+        pl.semaphore_wait(ready_sem, 11)
 
     for index in (5, 6, 7):
         scatter(0, x0, 0, index)
@@ -464,7 +481,7 @@
             pltpu.VMEM((2048, LANES), F32),
             pltpu.VMEM((256, LANES), F32),
             dma((8,)), dma, dma((2, 2, SIDE)), dma((2, 2, SIDE)), dma((2, 2, SIDE)), dma((2, 2, SIDE)),
-            dma((12,)), dma((4,)), dma((4,)), dma((4, 2)), dma((4,)), dma((4,)), dma((4,)), dma((3,)), dma((2,)),
+            dma((12,)), dma((4,)), dma((4,)), dma((4, 2)), dma((4,)), dma((4,)), dma((4,)), dma((3,)), dma((2,)), pltpu.SemaphoreType.REGULAR,
         ],
         compiler_params=pltpu.CompilerParams(collective_id=0, has_side_effects=True, vmem_limit_bytes=52 * MIB),
         cost_estimate=pl.CostEstimate(flops=2 * 2 * 2048 * 1024 * 128, bytes_accessed=18 * MIB, transcendentals=0),

time: 57.7 us -> 56.6 us (0.981)
  Pallas kernels: 56.8 us -> 55.2 us
    pallas_call x1, Pallas kernels: 55.6 us -> 54 us  [body(): pl.pallas_call(kernel, out_shape=(jax.ShapeDtypeStruct((2, 1024, LANES),...]
where the time goes in v6:
time: 56.6 us; the launch traced here: 55.8 us
  Pallas kernels  55.2 us (98%)
  between operations  0.64 us (1%)
    pallas_call x1, Pallas kernels, body(): pl.pallas_call(kernel, out_shape=(jax.ShapeDtypeStruct((2, 1024, LANES),...  54 us
    pallas_call x1, Pallas kernels, body(): pl.pallas_call(write_out, out_shape=tuple((jax.ShapeDtypeStruct(r.shape,...  1.17 us

profile of v6, /device:TPU:57, one launch (start us, length us, event | category | flops | bytes accessed | tf_op | source)
XLA Modules:
  0.0 55.8 jit_solution(14105991988100335079)
XLA Ops:
  0.6 54.0 %block_steps.1 = (f32[2,1024,128]{2,1,0:T(8,128)S(1)}, f32[1024,128]{1,0:T(8,128)S(1)}) custom-call(f32[2,2048,1024]{2,1,0:T(8,128)} %factor.1, f32[2,1024,2048]{2,1,0:T(8,128)} %inverses.1, f32[2048,128]{1,0:T(8,128)} %rhs.1), custom_call_target="tpu_custom_call" | custom-call | flops 1073741824 | bytes 18874368 | tf_op jit(solution)/shard_map/block_steps/pallas_call | solution.py:463
  54.6 1.2 %write_out.1 = (f32[2,1024,128]{2,1,0:T(8,128)}, f32[1024,128]{1,0:T(8,128)}) custom-call(f32[2,1024,128]{2,1,0:T(8,128)S(1)} %get-tuple-element.4.solved, f32[1024,128]{1,0:T(8,128)S(1)} %get-tuple-element.5.updated), custom_call_target="tpu_custom_call" | custom-call | bytes 3145728 | tf_op jit(solution)/shard_map/write_out/pallas_call | solution.py:490

commit v7 on v6

--- a/solution.py
+++ b/solution.py
@@ -42,6 +42,15 @@
     def at(yy, zz):
         return {"row": zz * SIDE + yy}
 
+    b_copy = pltpu.make_async_copy(rhs, b, b_sem)
+
+    @pl.when(is_first)
+    def _():
+        b_copy.start()
+        for block in range(4):
+            pltpu.make_async_copy(
+                inverses.at[0, pl.ds(block * 256, 256)], stage_wide.at[block], stage_sem.at[4 + block]).start()
+
     barrier = pltpu.get_barrier_semaphore()
 
     def greet(target):
@@ -49,7 +58,7 @@
         def _():
             pl.semaphore_signal(barrier, inc=1, device_id=target, device_id_type=MESH)
 
-    for k in FAR_FIRST:
+    for k in (1, 7, 4, 3, 5, 2, 6):
         greet(at(lax.rem(y + k, SIDE), z))
         greet(at(y, lax.rem(z + k, SIDE)))
 
@@ -135,16 +144,14 @@
         both = total[:256, :] + total[256:, :]
         return both[:, :LANES] + both[:, LANES:]
 
-    b_copy = pltpu.make_async_copy(rhs, b, b_sem)
-    b_copy.start()
-
-    @pl.when(is_first | is_second)
+    @pl.when(is_second)
     def _():
         for block in range(4):
             load_inverse(row, jnp.int32(block)).start()
 
     @pl.when(jnp.logical_not(is_first))
     def _():
+        b_copy.start()
         for block in range(4):
             load_factor(jnp.int32(block)).start()
 

time: 56.6 us -> 55.7 us (0.984)
  the two profiles are of different devices: /device:TPU:57 before, /device:TPU:65 now
where the time goes in v7:
time: 55.7 us; the launch traced here: 55.6 us
  Pallas kernels  55 us (99%)
  between operations  0.64 us (1%)
    pallas_call x1, Pallas kernels, body(): pl.pallas_call(kernel, out_shape=(jax.ShapeDtypeStruct((2, 1024, LANES),...  53.8 us
    pallas_call x1, Pallas kernels, body(): pl.pallas_call(write_out, out_shape=tuple((jax.ShapeDtypeStruct(r.shape,...  1.17 us

profile of v7, /device:TPU:65, one launch (start us, length us, event | category | flops | bytes accessed | tf_op | source)
XLA Modules:
  0.0 55.6 jit_solution(15472503890231654647)
XLA Ops:
  0.6 53.8 %block_steps.1 = (f32[2,1024,128]{2,1,0:T(8,128)S(1)}, f32[1024,128]{1,0:T(8,128)S(1)}) custom-call(f32[2,2048,1024]{2,1,0:T(8,128)} %factor.1, f32[2,1024,2048]{2,1,0:T(8,128)} %inverses.1, f32[2048,128]{1,0:T(8,128)} %rhs.1), custom_call_target="tpu_custom_call" | custom-call | flops 1073741824 | bytes 18874368 | tf_op jit(solution)/shard_map/block_steps/pallas_call | solution.py:470
  54.4 1.2 %write_out.1 = (f32[2,1024,128]{2,1,0:T(8,128)}, f32[1024,128]{1,0:T(8,128)}) custom-call(f32[2,1024,128]{2,1,0:T(8,128)S(1)} %get-tuple-element.4.solved, f32[1024,128]{1,0:T(8,128)S(1)} %get-tuple-element.5.updated), custom_call_target="tpu_custom_call" | custom-call | bytes 3145728 | tf_op jit(solution)/shard_map/write_out/pallas_call | solution.py:497
